TPU v7x, 256 devices: a whole 4x4x8 slice. The times are simulated.
256 devices in a mesh: section: 2 (over z_hi), dp: 16 (over z_lo, x), seq: 8 (over y, core).
Axes of the slice: x: 4, y: 4, z: 8 (z_hi: 2, z_lo: 4; z = z_hi * 4 + z_lo), core: 2. Of those that a mesh axis runs over, the one named last changes fastest.
Arguments:
- qkv_rows: bfloat16 [2, 16, 1024, 9216], P('section', 'dp', 'seq'), may hold values from -30 to 30
- gate: float32 [2, 16, 3072], P('section', 'dp'), may hold values from -4 to 4
- out_weight: bfloat16 [3072, 3072], P('seq'), may hold values from -0.109375 to 0.109375
- out_grad: bfloat16 [2, 16, 1024, 3072], P('section', 'dp', 'seq'), may hold values from -6 to 6
- tile_order: int32 [1024], replicated, may hold values from 0 to 1023, as said below
- window: int32 [16, 6], replicated, may hold values from 0 to 15, as said below
Outputs:
- gated_out: bfloat16 [2, 16, 1024, 3072], P('section', 'dp', 'seq')
- weight_grad: float32 [3072, 3072], P('seq', ('section', 'dp'))
- gate_grad: float32 [2, 16, 3072], P('section', 'dp')
Inputs may be any that keep to these rules, and one draw needn't show every extreme that they name: `tile_order`: lists every token once. `window`: row t names 6 different tiles, the first of them t itself.
All inputs are finite; a program needn't handle non-finite values.
Results may differ from a plain program's by a relative error of at most 0.023.
Values may be sent and summed in bfloat16 or wider, within the bound.
A program may use at most 128 MiB of HBM per device.

v0:
```python
import math

import jax
import jax.numpy as jnp
from jax import lax
from jax.sharding import PartitionSpec as P

HEADS = 24
TILE = 64


def shifted(value, axis, steps):
    count = lax.axis_size(axis)
    pairs = [(source, (source + steps) % count) for source in range(count)]
    return lax.ppermute(value, axis, pairs)


def attend_heads(by_heads, tile_order, window):
    token_count = by_heads.shape[0]
    head_count = by_heads.shape[2]
    head_dim = by_heads.shape[3]
    tile_count = token_count // TILE
    key_tiles = window.shape[1]
    tiled_rows = by_heads[tile_order].reshape(tile_count, TILE, 3, head_count, head_dim)
    scale_factor = 1.0 / math.sqrt(head_dim)

    def one_tile(tile_index):
        queries = tiled_rows[tile_index, :, 0]
        gathered = tiled_rows[window[tile_index]].reshape(key_tiles * TILE, 3, head_count, head_dim)
        scores = (
            jnp.einsum("qhd,khd->hqk", queries, gathered[:, 1], preferred_element_type=jnp.float32)
            * scale_factor
        )
        weights = jax.nn.softmax(scores, axis=-1).astype(jnp.bfloat16)
        mixed_rows = jnp.einsum(
            "hqk,khd->qhd", weights, gathered[:, 2], preferred_element_type=jnp.float32
        )
        return mixed_rows.astype(jnp.bfloat16)

    tiles_out = lax.map(one_tile, jnp.arange(tile_count, dtype=jnp.int32), batch_size=8)
    flat_rows = tiles_out.reshape(token_count, head_count * head_dim)
    return jnp.zeros_like(flat_rows).at[tile_order].set(flat_rows)


def attend_rows(rows, tile_order, window):
    local_tokens = rows.shape[2]
    head_dim = rows.shape[3] // (3 * HEADS)
    split_rows = rows.reshape(local_tokens, 3, HEADS, head_dim)
    by_heads = lax.all_to_all(split_rows, "seq", split_axis=2, concat_axis=0, tiled=True)
    return attend_heads(by_heads, tile_order, window)


def per_device(qkv_rows, gate, out_weight, out_grad, tile_order, window):
    local_tokens = qkv_rows.shape[2]
    model_width = out_grad.shape[3]
    arrived = shifted(qkv_rows, "section", 1)
    attended = attend_rows(arrived, tile_order, window)
    gate_row = gate.reshape(model_width)
    grad_rows = out_grad.reshape(local_tokens, model_width).astype(jnp.float32)
    rows_part = lax.slice_in_dim(attended, 0, local_tokens * lax.axis_size("seq"), axis=0)
    projected = lax.psum_scatter(
        jnp.dot(rows_part, out_weight, preferred_element_type=jnp.float32).astype(jnp.bfloat16),
        "seq",
        scatter_dimension=0,
        tiled=True,
    ).astype(jnp.float32)
    gated_out = (gate_row * projected).astype(jnp.bfloat16).reshape(1, 1, local_tokens, model_width)
    gate_grad = lax.psum(jnp.sum(grad_rows * projected, axis=0), "seq")
    proj_grad = (gate_row * grad_rows).astype(jnp.bfloat16)
    zero_grad = jnp.zeros((attended.shape[1], model_width), jnp.float32)
    block_rows = lax.all_gather(proj_grad, "seq", axis=0, tiled=True)
    matching = lax.slice_in_dim(attended, 0, block_rows.shape[0], axis=0)
    partial_grad = zero_grad + lax.dot_general(
        matching, block_rows, (((0,), (0,)), ((), ())), preferred_element_type=jnp.float32
    )
    weight_grad = lax.psum_scatter(
        partial_grad.astype(jnp.bfloat16), ("section", "dp"), scatter_dimension=1, tiled=True
    ).astype(jnp.float32)
    return (gated_out, weight_grad, gate_grad.reshape(1, 1, model_width))


def solution(mesh):
    placed = (
        P("section", "dp", "seq", None),
        P("section", "dp", None),
        P("seq", None),
        P("section", "dp", "seq", None),
        P(),
        P(),
    )
    return jax.shard_map(
        per_device,
        mesh=mesh,
        in_specs=placed,
        out_specs=(
            P("section", "dp", "seq", None),
            P("seq", ("section", "dp")),
            P("section", "dp", None),
        ),
        check_vma=False,
    )
```

profile of v0, /device:TPU:1, one launch (start us, length us, event | category | flops | bytes accessed | tf_op | source)
XLA Modules:
  0.0 571.2 jit_solution(6944856568759564084)
XLA Ops:
  7.2 4.4 copy.30
  11.6 7.7 %collective-permute-start = (bf16[1,1,128,9216]{2,3,1,0:T(8,128)(2,1)}, bf16[1,1,128,9216]{2,3,1,0:T(8,128)(2,1)S(1)}, u32[]{:S(2)}, u32[]{:S(2)}) collective-permute-start(bf16[1,1,128,9216]{2,3,1,0:T(8,128)(2,1)} %copy.30), channel_id=1, source_target_pairs={{0,128},{128,0},{1,129},{129,1},{2,130},{130,2},{3,131},{131,3},{4... | collective-permute-start | bytes 7077896 | tf_op jit(solution)/shard_map/ppermute | solution.py:15
  19.4 71.0 %collective-permute-done = bf16[1,1,128,9216]{2,3,1,0:T(8,128)(2,1)S(1)} collective-permute-done((bf16[1,1,128,9216]{2,3,1,0:T(8,128)(2,1)}, bf16[1,1,128,9216]{2,3,1,0:T(8,128)(2,1)S(1)}, u32[]{:S(2)}, u32[]{:S(2)}) %collective-permute-start) | collective-permute-done | bytes 2359328 | tf_op jit(solution)/shard_map/ppermute | solution.py:15
  90.4 1.6 copy.31
  91.9 35.8 %all-to-all-start = ((bf16[128,3,24,128]{0,3,1,2:T(8,128)(2,1)}), bf16[128,3,24,128]{0,3,1,2:T(8,128)(2,1)}, u32[]{:S(2)}, u32[]{:S(2)}) async-start(bf16[128,3,24,128]{0,3,1,2:T(8,128)(2,1)} %copy.31), calls=%async_computation | async-start | bytes 4718592 | tf_op jit(solution)/shard_map/all_to_all | solution.py:49
  127.7 0.1 copy.36
  127.8 29.1 %all-to-all-done = bf16[128,3,24,128]{0,3,1,2:T(8,128)(2,1)} async-done(((bf16[128,3,24,128]{0,3,1,2:T(8,128)(2,1)}), bf16[128,3,24,128]{0,3,1,2:T(8,128)(2,1)}, u32[]{:S(2)}, u32[]{:S(2)}) %all-to-all-start) | async-done | bytes 2359328 | tf_op jit(solution)/shard_map/all_to_all | solution.py:49
  157.0 4.3 copy.33
  161.3 5.3 copy.34
  166.6 12.3 %gather_fusion.3 = bf16[1024,3,3,128]{3,2,1,0:T(4,128)(2,1)} fusion(bf16[1024,3,3,128]{3,2,1,0:T(4,128)(2,1)} %copy.34, s32[1024]{0:T(1024)S(1)} %get-tuple-element.68), kind=kCustom, calls=%fused_computation.3 | custom fusion | bytes 4722688 | tf_op jit(solution)/shard_map/gather | solution.py:24
  178.9 4.0 copy.37
  182.9 52.9 %while.10 = (s32[]{:T(128)}, bf16[2,8,64,3,128]{4,2,3,1,0:T(8,128)(2,1)S(1)}, s32[2,8]{1,0:T(2,128)S(1)}, s32[16,6]{1,0:T(8,128)S(1)}, bf16[16,64,3,3,128]{4,1,3,2,0:T(8,128)(2,1)}, /*index=5*/s32[]{:T(128)}) while((s32[]{:T(128)}, bf16[2,8,64,3,128]{4,2,3,1,0:T(8,128)(2,1)S(1)}, s32[2,8]{1,0:T(2,128)S(1)}, s32[16,6]{1,0:T(8,128)S(1)}, ...), condition=%wide.region_3.4_spmd, body=%wide.region_0.3_spmd.sunk | while | flops 305727040 | bytes 62943680 | solution.py:40
  182.9 0.5 copy-done.7
  183.5 0.6 gather_fusion
  184.0 0.1 reshape.160
  184.1 7.0 %gather_fusion.1 = bf16[48,64,3,3,128]{4,1,3,2,0:T(8,128)(2,1)} fusion(bf16[16,64,3,3,128]{4,1,3,2,0:T(8,128)(2,1)} %get-tuple-element.125, s32[1024]{0:T(1024)S(1)} %pad_clamp_fusion.2), kind=kCustom, calls=%fused_computation.1.clone.1 | custom fusion | bytes 14155968 | tf_op jit(solution)/shard_map/while/body/eval_jaxpr/vmap()/gather | solution.py:29
  191.2 5.4 copy.64
  196.6 2.4 fusion.38
  199.0 2.3 gather_fusion.2
  201.3 2.8 fusion.39
  204.2 4.4 fusion.40
  208.6 0.8 fusion.41
  209.4 0.5 copy-done.7
  209.9 0.6 gather_fusion
  210.5 0.1 reshape.160
  210.6 7.0 %gather_fusion.1 = bf16[48,64,3,3,128]{4,1,3,2,0:T(8,128)(2,1)} fusion(bf16[16,64,3,3,128]{4,1,3,2,0:T(8,128)(2,1)} %get-tuple-element.125, s32[1024]{0:T(1024)S(1)} %pad_clamp_fusion.2), kind=kCustom, calls=%fused_computation.1.clone.1 | custom fusion | bytes 14155968 | tf_op jit(solution)/shard_map/while/body/eval_jaxpr/vmap()/gather | solution.py:29
  217.6 5.4 copy.64
  223.1 2.4 fusion.38
  225.5 2.3 gather_fusion.2
  227.8 2.8 fusion.39
  230.6 4.4 fusion.40
  235.0 0.8 fusion.41
  235.9 0.9 copy-done.2
  236.7 1.8 copy.38
  238.6 6.1 %scatter_custom_fusion = bf16[1024,384]{1,0:T(8,128)(2,1)} fusion(s32[1024]{0:T(1024)S(1)} %get-tuple-element.69, bf16[128,8,3,128]{3,2,1,0:T(4,128)(2,1)S(1)} %bitcast.70, bf16[]{:T(256)} %constant.19.clone.1), kind=kCustom, calls=%fused_computation.35 | custom fusion | bytes 1835010 | tf_op jit(solution)/shard_map/scatter | solution.py:42
  244.6 6.6 %convolution_convert_fusion = bf16[1024,3072]{1,0:T(8,128)(2,1)} fusion(bf16[1024,384]{1,0:T(8,128)(2,1)} %scatter_custom_fusion, bf16[384,3072]{1,0:T(8,128)(2,1)S(1)} %copy-done), kind=kOutput, calls=%fused_computation.26 | convolution fusion | flops 2419064832 | bytes 9437184 | tf_op jit(solution)/shard_map/dot_general | solution.py:62
  251.2 0.0 reduce-scatter.3.cloned.1.call-update
  251.2 0.0 all-gather.2.cloned.1.call-start
  251.3 44.8 %reduce-scatter.3.cloned.1.call-done = bf16[128,3072]{1,0:T(8,128)(2,1)} async-done(((bf16[1024,3072]{1,0:T(8,128)(2,1)}), bf16[128,3072]{1,0:T(8,128)(2,1)}) %reduce-scatter.3.cloned.1.call-update) | async-done | bytes 786448 | tf_op jit(solution)/shard_map/reduce_scatter | solution.py:61
  296.1 2.9 fusion.17
  299.0 0.0 all-gather.2.cloned.1.call-update
  299.0 0.0 reduce-scatter.5.cloned.1.call-start
  299.1 44.3 %all-gather.2.cloned.1.call-done = bf16[1024,3072]{1,0:T(8,128)(2,1)} async-done(((bf16[128,3072]{1,0:T(8,128)(2,1)}), bf16[1024,3072]{1,0:T(8,128)(2,1)}) %all-gather.2.cloned.1.call-update) | async-done | bytes 6291472 | tf_op jit(solution)/shard_map/all_gather | solution.py:71
  343.4 7.7 %convolution_convert_fusion.1 = bf16[384,3072]{0,1:T(8,128)(2,1)} fusion(bf16[1024,384]{1,0:T(8,128)(2,1)S(1)} %copy-done.3, bf16[1024,3072]{1,0:T(8,128)(2,1)} %all-gather.2.cloned.1.call-done), kind=kOutput, calls=%fused_computation.27 | convolution fusion | flops 2417098752 | bytes 9437184 | tf_op jit(solution)/shard_map/dot_general | solution.py:73
  351.1 0.0 reduce-scatter.5.cloned.1.call-update
  351.1 21.2 %psum.7 = f32[1,1,3072]{2,1,0:T(1,128)} all-reduce(f32[1,1,3072]{2,1,0:T(1,128)S(1)} %bitcast.72), channel_id=1, replica_groups=mesh['section'=2,'dp'=16,'seq'=8] {'seq'}, use_global_device_ids=true, to_apply=%region_8.9 | all-reduce | flops 3072 | bytes 24576 | tf_op jit(solution)/shard_map/psum | solution.py:68
  372.3 190.8 %reduce-scatter.5.cloned.1.call-done = bf16[384,96]{0,1:T(8,128)(2,1)} async-done(((bf16[384,3072]{0,1:T(8,128)(2,1)}), bf16[384,96]{0,1:T(8,128)(2,1)}) %reduce-scatter.5.cloned.1.call-update) | async-done | bytes 73744 | tf_op jit(solution)/shard_map/reduce_scatter | solution.py:76
  563.1 1.6 convert_element_type.40
  (31 shorter events, 0.1 us)
Async XLA Ops:
  7.2 237.5 %copy-start = (bf16[384,3072]{1,0:T(8,128)(2,1)S(1)}, bf16[384,3072]{1,0:T(8,128)(2,1)}, u32[]{:S(2)}) copy-start(bf16[384,3072]{1,0:T(8,128)(2,1)} %param.10) | copy-start | bytes 7077892
  11.6 78.7 %collective-permute-start = (bf16[1,1,128,9216]{2,3,1,0:T(8,128)(2,1)}, bf16[1,1,128,9216]{2,3,1,0:T(8,128)(2,1)S(1)}, u32[]{:S(2)}, u32[]{:S(2)}) collective-permute-start(bf16[1,1,128,9216]{2,3,1,0:T(8,128)(2,1)} %copy.30), channel_id=1, source_target_pairs={{0,128},{128,0},{1,129},{129,1},{2,130},{130,2},{3,131},{131,3},{4... | collective-permute-start | bytes 7077896 | tf_op jit(solution)/shard_map/ppermute | solution.py:15
  91.9 35.8 %copy-start.5 = (s32[16,6]{0,1:T(8,128)S(1)}, s32[16,6]{0,1:T(8,128)}, u32[]{:S(2)}) copy-start(s32[16,6]{0,1:T(8,128)} %param.13) | copy-start | bytes 1156
  91.9 35.9 %copy-start.6 = (s32[1024]{0:T(1024)S(1)}, s32[1024]{0:T(1024)}, u32[]{:S(2)}) copy-start(s32[1024]{0:T(1024)} %param.12) | copy-start | bytes 12292
  91.9 65.0 %all-to-all-start = ((bf16[128,3,24,128]{0,3,1,2:T(8,128)(2,1)}), bf16[128,3,24,128]{0,3,1,2:T(8,128)(2,1)}, u32[]{:S(2)}, u32[]{:S(2)}) async-start(bf16[128,3,24,128]{0,3,1,2:T(8,128)(2,1)} %copy.31), calls=%async_computation | async-start | bytes 4718592 | tf_op jit(solution)/shard_map/all_to_all | solution.py:49
  127.7 168.4 %reduce-scatter.3.cloned.1.call-start = ((), (), s32[]{:S(2)}) async-start(), calls=%async_computation.3 | async-start | bytes 7077888 | tf_op jit(solution)/shard_map/reduce_scatter | solution.py:61
  182.9 0.6 copy-start.7
  204.2 4.4 copy-start.1
  208.5 0.8 copy-start.8
  209.4 0.6 copy-start.7
  230.6 4.4 copy-start.1
  235.0 0.8 copy-start.8
  235.9 0.9 copy-start.2
  251.2 44.9 %copy-start.4 = (f32[1,1,3072]{2,1,0:T(1,128)S(1)}, f32[1,1,3072]{2,1,0:T(1,128)}, u32[]{:S(2)}) copy-start(f32[1,1,3072]{2,1,0:T(1,128)} %param.9) | copy-start | bytes 36868
  251.2 92.2 %copy-start.3 = (bf16[1024,384]{1,0:T(8,128)(2,1)S(1)}, bf16[1024,384]{1,0:T(8,128)(2,1)}, u32[]{:S(2)}) copy-start(bf16[1024,384]{1,0:T(8,128)(2,1)} %scatter_custom_fusion) | copy-start | bytes 2359300
  251.2 92.2 %all-gather.2.cloned.1.call-start = ((), (), s32[]{:S(2)}) async-start(), calls=%async_computation.4 | async-start | bytes 7077888 | tf_op jit(solution)/shard_map/all_gather | solution.py:71
  299.0 264.1 %reduce-scatter.5.cloned.1.call-start = ((), (), s32[]{:S(2)}) async-start(), calls=%async_computation.5 | async-start | bytes 2433024 | tf_op jit(solution)/shard_map/reduce_scatter | solution.py:76
Sparse Core Ops, SparseCore 0:
  251.3 44.7 reduce-scatter.2
  299.1 44.2 all-gather.1
  351.2 211.7 reduce-scatter.4
where the time goes:
time: 576 us; the launch traced here: 571 us
  waiting for transfers between devices  380 us (66%)
  local copies, waits for them, and re-layouts  77.6 us (13%)
  starting transfers between devices  43.6 us (8%)
  matrix products  21.5 us (4%)
  blocking collectives  21.2 us (4%)
  between operations  13.8 us (2%)
  other arithmetic  13.2 us (2%)
    reduce_scatter x1, waiting for transfers between devices, per_device(): lax.psum_scatter(partial_grad.astype(jnp.bfloat16), ('section', 'dp'), sc...  191 us
    ppermute x1, waiting for transfers between devices, shifted(): return lax.ppermute(value, axis, pairs)  71 us
    reduce_scatter x1, waiting for transfers between devices, per_device(): lax.psum_scatter(jnp.dot(rows_part, out_weight, preferred_element_type=jn...  44.8 us
    all_gather x1, waiting for transfers between devices, per_device(): block_rows = lax.all_gather(proj_grad, 'seq', axis=0, tiled=True)  44.3 us
    all_to_all x1, starting transfers between devices, attend_rows(): lax.all_to_all(split_rows, 'seq', split_axis=2, concat_axis=0, tiled=True)  35.8 us
    all_to_all x1, waiting for transfers between devices, attend_rows(): lax.all_to_all(split_rows, 'seq', split_axis=2, concat_axis=0, tiled=True)  29.1 us
    gather x4, local copies, waits for them, and re-layouts, one_tile(): tiled_rows[window[tile_index]]  24.9 us
    psum x1, blocking collectives, per_device(): gate_grad = lax.psum(jnp.sum(grad_rows * projected, axis=0), 'seq')  21.2 us
  transfers between devices with their start and end apart: 5, of which 5 were waited for; matrix products, arithmetic and copies ran while one was open for 0% of the time, Pallas kernels for 0%

commit v1 on v0

v1 whole, which is shorter than its diff:
```python
import functools
import math

import jax
import jax.numpy as jnp
from jax import lax
from jax.experimental import pallas as pl
from jax.experimental.pallas import tpu as pltpu
from jax.sharding import PartitionSpec as P

MESH = pl.DeviceIdType.MESH
TILE = 64
HEAD = 128
BF = jnp.bfloat16
F32 = jnp.float32
MASKED = -(2.0**30)
NY, NX, NZ, NQ = 4, 4, 8, 8
HEADS_HERE = 3


def kernel(
    qkv, gate, weight, grad, order, window,
    gated_out, wgrad_out, ggrad_out,
    qkv_v, qx, kx, att_v, att_r, w_v, grad_v, pg, part, rs_s, rs_r, gg,
    own, ex_s, ex_r, zs, zr, xs, xr, xown,
    local_sem, a2a_s, a2a_r, swap_s, swap_r, w_s, w_r, ag_s, ag_r, y_s, y_r,
    gg_s, gg_r, ex_ss, ex_rs, z_s, z_r, x_s, x_r,
):
    sec, dp, q = lax.axis_index("section"), lax.axis_index("dp"), lax.axis_index("seq")
    zl, x = dp // NX, dp % NX
    y, c = q // 2, q % 2
    z = sec * (NZ // 2) + zl
    rows = qkv.shape[0]
    width = grad.shape[1]
    feats = HEADS_HERE * HEAD

    def at_seq(j):
        return {"seq": j}

    def at_y(dy):
        return {"seq": ((y + dy) % NY) * 2 + c}

    def at_z(dz):
        there = (z + dz) % NZ
        return {"section": there // (NZ // 2), "dp": (there % (NZ // 2)) * NX + x}

    def at_x(dx):
        return {"dp": zl * NX + (x + dx) % NX}

    def opposite(core):
        return {"section": 1 - sec, "seq": y * 2 + core}

    other = {"seq": y * 2 + 1 - c}

    def send(src, dst, s_sem, r_sem, where):
        copy = pltpu.make_async_remote_copy(
            src_ref=src, dst_ref=dst, send_sem=s_sem, recv_sem=r_sem, device_id=where, device_id_type=MESH
        )
        copy.start()

    def landed(ref, sem):
        pltpu.make_async_copy(ref, ref, sem).wait()

    barrier = pltpu.get_barrier_semaphore()
    partners = [at_seq((q + k) % NQ) for k in range(1, NQ)]
    partners += [opposite(0), opposite(1), at_z(1), at_z(NZ - 1)]
    partners += [at_x(k) for k in range(1, NX)]
    for partner in partners:
        pl.semaphore_signal(barrier, inc=1, device_id=partner, device_id_type=MESH)
    pl.semaphore_wait(barrier, len(partners))

    mine = pl.ds(pl.multiple_of(q * rows, rows), rows)
    for head in range(HEADS_HERE):
        for what in range(3):

            def columns(j):
                return pl.ds(pl.multiple_of(what * width + j * feats + head * HEAD, HEAD), HEAD)

            def one_peer(k, carry):
                j = (q + k) % NQ
                send(
                    qkv.at[:, columns(j)], qkv_v.at[head, what, mine, :], a2a_s, a2a_r.at[head], at_seq(j)
                )
                return carry

            lax.fori_loop(1, NQ, one_peer, 0)
            pltpu.make_async_copy(
                qkv.at[:, columns(q)], qkv_v.at[head, what, mine, :], local_sem.at[head]
            ).start()

    send(weight, w_v.at[pl.ds(feats, feats), :], w_s, w_r, other)
    pltpu.make_async_copy(weight, w_v.at[pl.ds(0, feats), :], local_sem.at[3]).start()
    pltpu.make_async_copy(grad, grad_v, local_sem.at[4]).start()

    slot_tile = lax.broadcasted_iota(jnp.int32, (NQ * rows, HEAD), 0) >> 6
    in_tile = jnp.where(slot_tile == lax.broadcasted_iota(jnp.int32, (NQ * rows, HEAD), 1), 1.0, 0.0).astype(BF)
    tiles = window.shape[0]
    tile_ids = lax.broadcasted_iota(jnp.int32, (tiles, HEAD), 1)
    chosen = tile_ids == window[:, 0:1]
    for k in range(1, window.shape[1]):
        chosen = jnp.logical_or(chosen, tile_ids == window[:, k : k + 1])
    bias = jnp.where(chosen, 0.0, MASKED)
    bias = jnp.concatenate([bias, jnp.zeros((HEAD - tiles, HEAD), F32)], axis=0).astype(BF)
    for part_of in range(NY):
        here = pl.ds(part_of * 2 * rows, 2 * rows)
        tokens = lax.broadcasted_iota(jnp.int32, (2 * rows, NQ * rows), 0) + part_of * 2 * rows
        placed = jnp.where(tokens == order[...], 1.0, 0.0).astype(BF)
        tile_of = jnp.dot(placed, in_tile, preferred_element_type=F32).astype(BF)
        kx[here, :] = tile_of
        qx[here, :] = jnp.dot(tile_of, bias, preferred_element_type=F32).astype(BF)

    pltpu.make_async_copy(grad, grad_v, local_sem.at[4]).wait()
    pg[y] = (gate[...] * grad_v[...].astype(F32)).astype(BF)

    scale = 1.0 / math.sqrt(HEAD)
    for head in range(HEADS_HERE):
        landed(qkv_v.at[head, :, pl.ds(0, (NQ - 1) * rows), :], a2a_r.at[head])
        landed(qkv_v.at[head, :, pl.ds(0, rows), :], local_sem.at[head])
        if head == HEADS_HERE - 1:
            send(pg.at[y], pg.at[y], ag_s.at[0], ag_r.at[0], at_y(1))
            send(pg.at[y], pg.at[y], ag_s.at[1], ag_r.at[1], at_y(NY - 1))

        def attend(chunk, carry):
            here = pl.ds(pl.multiple_of(chunk * 2 * rows, 2 * rows), 2 * rows)
            queries = jnp.concatenate([qkv_v[head, 0, here, :], qx[here, :]], axis=1)
            keys = jnp.concatenate([qkv_v[head, 1], kx[...]], axis=1)
            scores = lax.dot_general(
                queries, keys, (((1,), (1,)), ((), ())), preferred_element_type=F32
            )
            top = jnp.max(scores, axis=1, keepdims=True)
            powers = jnp.exp((scores - top) * scale)
            total = jnp.sum(powers, axis=1, keepdims=True)
            mixed = jnp.dot(powers.astype(BF), qkv_v[head, 2], preferred_element_type=F32) / total
            att_v[head, chunk] = mixed.astype(BF).reshape(2, rows, HEAD)
            send(
                att_v.at[head, chunk, c],
                att_r.at[chunk, :, pl.ds(head * HEAD, HEAD)],
                swap_s, swap_r.at[head], opposite(c),
            )
            send(
                att_v.at[head, chunk, 1 - c],
                att_r.at[chunk, :, pl.ds(feats + head * HEAD, HEAD)],
                swap_s, swap_r.at[head], opposite(1 - c),
            )
            return carry

        lax.fori_loop(0, NY, attend, 0)

    left, right = (y + NY - 1) % NY, (y + 1) % NY
    half = rows // 2
    landed(pg.at[left], ag_r.at[0])
    send(pg.at[left, pl.ds(0, half)], pg.at[left, pl.ds(0, half)], ag_s.at[2], ag_r.at[2], at_y(1))
    landed(pg.at[right], ag_r.at[1])
    send(pg.at[right, pl.ds(half, half)], pg.at[right, pl.ds(half, half)], ag_s.at[3], ag_r.at[3], at_y(NY - 1))

    landed(w_v.at[pl.ds(0, feats), :], local_sem.at[3])
    landed(w_v.at[pl.ds(0, feats), :], w_r)
    for head in range(HEADS_HERE):
        landed(att_r.at[:, :, pl.ds(0, 2 * HEAD)], swap_r.at[head])

    def project(tile, carry):
        cols = pl.ds(pl.multiple_of(tile * 256, 256), 256)
        part[:, :, cols] = jnp.dot(
            att_r[...].reshape(NY * rows, 2 * feats), w_v[:, cols], preferred_element_type=F32
        ).reshape(NY, rows, 256)
        return carry

    lax.fori_loop(0, width // 256, project, 0)

    far = (y + 2) % NY
    landed(pg.at[far, pl.ds(0, half)], ag_r.at[2])
    landed(pg.at[far, pl.ds(0, half)], ag_r.at[3])

    group = width // 4
    first_column = (0, 2 * group, group, 3 * group)

    def y_step(k):
        for ch in range(4):
            up = ch % 2 == 0
            block = (y + 2 * NY - 1 - k) % NY if up else (y + 1 + k) % NY
            cols = pl.ds(first_column[ch], group)
            value = part[block, :, cols]
            if k > 0:
                landed(rs_r.at[ch, k - 1], y_r.at[ch, k - 1])
                value = value + rs_r[ch, k - 1].astype(F32)
            if k < NY - 1:
                rs_s[ch, k] = value.astype(BF)
                send(
                    rs_s.at[ch, k], rs_r.at[ch, k], y_s.at[ch, k], y_r.at[ch, k], at_y(1 if up else NY - 1)
                )
            else:
                gated_out[:, cols] = (gate[:, cols] * value).astype(BF)
                gg[q, :, cols] = jnp.sum(grad_v[:, cols].astype(F32) * value, axis=0, keepdims=True)

    y_step(0)

    zcols = width // NZ
    xcols = zcols // NX

    def wgrad(i, carry):
        sign = 2 * (i % 2) - 1
        block = (z + NZ + sign * (i // 2 + 1) * (1 - i // 7)) % NZ
        cols = pl.ds(pl.multiple_of(block * zcols, HEAD), zcols)
        product = lax.dot_general(
            pg[:, :, cols].reshape(NY * rows, zcols),
            att_r[...].reshape(NY * rows, 2 * feats),
            (((0,), (0,)), ((), ())),
            preferred_element_type=F32,
        )
        own[block] = product[:, :feats].reshape(NX, xcols, feats)
        ex_s[block] = product[:, feats:].astype(BF).reshape(NX, xcols, feats)
        send(ex_s.at[block], ex_r.at[block], ex_ss, ex_rs.at[i], other)
        return carry

    def exchanged(i):
        landed(ex_r.at[0], ex_rs.at[i])

    z_chains = ((2, 1), (3, -1), (1, 1), (0, -1))

    def z_step(k):
        if k < 4:
            exchanged(2 * k)
            exchanged(2 * k + 1)
        for ch, (j, way) in enumerate(z_chains):
            xb = (x + j) % NX
            block = (z + 2 * NZ - way * (1 + k)) % NZ
            value = own[block, xb] + ex_r[block, xb].astype(F32)
            if k > 0:
                landed(zr.at[ch, k - 1], z_r.at[ch, k - 1])
                value = value + zr[ch, k - 1].astype(F32)
            if k < NZ - 1:
                zs[ch, k] = value.astype(BF)
                send(
                    zs.at[ch, k], zr.at[ch, k], z_s.at[ch, k], z_r.at[ch, k], at_z(1 if way > 0 else NZ - 1)
                )
            elif j > 0:
                xs[j - 1] = value.astype(BF)
                send(xs.at[j - 1], xr.at[j - 1], x_s.at[j - 1], x_r.at[j - 1], at_x(j))
            else:
                xown[...] = value

    lax.fori_loop(0, 4, wgrad, 0)
    z_step(0)
    lax.fori_loop(4, 8, wgrad, 0)
    z_step(1)
    y_step(1)
    z_step(2)
    z_step(3)
    y_step(2)
    z_step(4)
    z_step(5)
    y_step(3)

    def gate_sums(k, carry):
        send(gg.at[q], gg.at[q], gg_s, gg_r, at_seq((q + k) % NQ))
        return carry

    lax.fori_loop(1, NQ, gate_sums, 0)
    z_step(6)
    z_step(7)

    landed(gg.at[pl.ds(0, NQ - 1)], gg_r)
    total = gg[0]
    for k in range(1, NQ):
        total = total + gg[k]
    ggrad_out[...] = total

    value = xown[...]
    for j in range(NX - 1):
        landed(xr.at[j], x_r.at[j])
        value = value + xr[j].astype(F32)
    wgrad_out[...] = value

    landed(qkv_v.at[:, :, pl.ds(0, (NQ - 1) * rows), :], a2a_s)
    landed(att_v, swap_s)
    landed(w_v.at[pl.ds(0, feats), :], w_s)
    for k in range(2):
        landed(pg.at[0], ag_s.at[k])
        landed(pg.at[0, pl.ds(0, half)], ag_s.at[2 + k])
    for ch in range(4):
        for k in range(NY - 1):
            landed(rs_s.at[ch, k], y_s.at[ch, k])
        for k in range(NZ - 1):
            landed(zs.at[ch, k], z_s.at[ch, k])
    landed(gg.at[pl.ds(0, NQ - 1)], gg_s)
    landed(ex_s, ex_ss)
    for j in range(NX - 1):
        landed(xs.at[j], x_s.at[j])


def per_device(qkv_rows, gate, out_weight, out_grad, tile_order, window):
    rows, wide = qkv_rows.shape[2:]
    width = out_grad.shape[3]
    feats = HEADS_HERE * HEAD
    tokens = rows * NQ
    zcols = width // NZ
    xcols = zcols // NX
    group = width // 4
    vmem = pl.BlockSpec(memory_space=pltpu.VMEM)
    anywhere = pl.BlockSpec(memory_space=pl.ANY)
    dma = pltpu.SemaphoreType.DMA
    scratch = [
        pltpu.VMEM((HEADS_HERE, 3, tokens, HEAD), BF),
        pltpu.VMEM((tokens, HEAD), BF),
        pltpu.VMEM((tokens, HEAD), BF),
        pltpu.VMEM((HEADS_HERE, NY, 2, rows, HEAD), BF),
        pltpu.VMEM((NY, rows, 2 * feats), BF),
        pltpu.VMEM((2 * feats, width), BF),
        pltpu.VMEM((rows, width), BF),
        pltpu.VMEM((NY, rows, width), BF),
        pltpu.VMEM((NY, rows, width), F32),
        pltpu.VMEM((4, NY - 1, rows, group), BF),
        pltpu.VMEM((4, NY - 1, rows, group), BF),
        pltpu.VMEM((NQ, 1, width), F32),
        pltpu.VMEM((NZ, NX, xcols, feats), F32),
        pltpu.VMEM((NZ, NX, xcols, feats), BF),
        pltpu.VMEM((NZ, NX, xcols, feats), BF),
        pltpu.VMEM((4, NZ - 1, xcols, feats), BF),
        pltpu.VMEM((4, NZ - 1, xcols, feats), BF),
        pltpu.VMEM((NX - 1, xcols, feats), BF),
        pltpu.VMEM((NX - 1, xcols, feats), BF),
        pltpu.VMEM((xcols, feats), F32),
        dma((5,)), dma(()), dma((HEADS_HERE,)), dma(()), dma((HEADS_HERE,)), dma(()), dma(()),
        dma((4,)), dma((4,)), dma((4, NY - 1)), dma((4, NY - 1)), dma(()), dma(()), dma(()), dma((NZ,)),
        dma((4, NZ - 1)), dma((4, NZ - 1)), dma((NX - 1,)), dma((NX - 1,)),
    ]
    gated_out, wgrad, ggrad = pl.pallas_call(
        kernel,
        out_shape=(
            jax.ShapeDtypeStruct((rows, width), BF),
            jax.ShapeDtypeStruct((xcols, feats), F32),
            jax.ShapeDtypeStruct((1, width), F32),
        ),
        in_specs=[anywhere, vmem, anywhere, anywhere, vmem, vmem],
        out_specs=(vmem, vmem, vmem),
        scratch_shapes=scratch,
        compiler_params=pltpu.CompilerParams(
            collective_id=0, has_side_effects=True, vmem_limit_bytes=56 * 2**20
        ),
    )(
        qkv_rows.reshape(rows, wide),
        gate.reshape(1, width),
        out_weight,
        out_grad.reshape(rows, width),
        tile_order.reshape(1, tokens),
        window,
    )
    return (
        gated_out.reshape(1, 1, rows, width),
        wgrad.T,
        ggrad.reshape(1, 1, width),
    )


def solution(mesh):
    placed = (
        P("section", "dp", "seq", None),
        P("section", "dp", None),
        P("seq", None),
        P("section", "dp", "seq", None),
        P(),
        P(),
    )
    return jax.shard_map(
        per_device,
        mesh=mesh,
        in_specs=placed,
        out_specs=(
            P("section", "dp", "seq", None),
            P("seq", ("section", "dp")),
            P("section", "dp", None),
        ),
        check_vma=False,
    )
```

time: 576 us -> 114 us (0.20)
  waiting for transfers between devices: 380 us -> 0 us
  Pallas kernels: 0 us -> 105 us
  local copies, waits for them, and re-layouts: 77.6 us -> 6.31 us
  starting transfers between devices: 43.6 us -> 0 us
  matrix products: 21.5 us -> 0 us
  blocking collectives: 21.2 us -> 0 us
  other arithmetic: 13.2 us -> 0 us
  between operations: 13.8 us -> 0.64 us
    reduce_scatter x2 -> x0, waiting for transfers between devices: 236 us -> none  [the longest x1 191 us: per_device(): lax.psum_scatter(partial_grad.astype(jnp.bfloat16), ('section', 'dp'), sc...]
    pallas_call x0 -> x1, Pallas kernels: none -> 105 us  [per_device(): pl.pallas_call(kernel, out_shape=(jax.ShapeDtypeStruct((rows, width), BF)...]
    ppermute x1 -> x0, waiting for transfers between devices: 71 us -> none  [shifted(): return lax.ppermute(value, axis, pairs)]
    all_gather x1 -> x0, waiting for transfers between devices: 44.3 us -> none  [per_device(): block_rows = lax.all_gather(proj_grad, 'seq', axis=0, tiled=True)]
    gather x9 -> x0, local copies, waits for them, and re-layouts: 42.9 us -> none  [the longest x4 24.9 us: one_tile(): tiled_rows[window[tile_index]]]
    all_to_all x1 -> x0, starting transfers between devices: 35.8 us -> none  [attend_rows(): lax.all_to_all(split_rows, 'seq', split_axis=2, concat_axis=0, tiled=True)]
    all_to_all x1 -> x0, waiting for transfers between devices: 29.1 us -> none  [attend_rows(): lax.all_to_all(split_rows, 'seq', split_axis=2, concat_axis=0, tiled=True)]
    dot_general x6 -> x0, matrix products: 21.5 us -> none  [the longest x1 7.71 us: per_device(): lax.dot_general(matching, block_rows, (((0,), (0,)), ((), ())), preferred...]
  transfers between devices with their start and end apart: 5 -> 0, of which waited for: 5 -> 0; matrix products, arithmetic and copies ran while one was open for 0% -> 0% of each run, Pallas kernels for 0% -> 0%
where the time goes in v1:
time: 114 us; the launch traced here: 112 us
  Pallas kernels  105 us (92%)
  local copies, waits for them, and re-layouts  6.31 us (6%)
    pallas_call x1, Pallas kernels, per_device(): pl.pallas_call(kernel, out_shape=(jax.ShapeDtypeStruct((rows, width), BF)...  105 us
    unnamed x4, local copies, waits for them, and re-layouts  6.31 us

profile of v1, /device:TPU:1, one launch (start us, length us, event | category | flops | bytes accessed | tf_op | source)
XLA Modules:
  0.0 112.0 jit_solution(2713505132190188208)
XLA Ops:
  0.6 1.4 %copy.9.window = s32[16,6]{1,0:T(8,128)} copy(s32[16,6]{0,1:T(8,128)} %param.11) | data formatting | bytes 768 | tf_op args[5]
  2.0 105.1 %shard_map.85 = (bf16[128,3072]{1,0:T(8,128)(2,1)}, f32[96,384]{1,0:T(8,128)}, f32[1,3072]{1,0:T(1,128)}) custom-call(bf16[128,9216]{1,0:T(8,128)(2,1)} %bitcast.7, f32[1,3072]{1,0:T(1,128)} %bitcast.12, bf16[384,3072]{1,0:T(8,128)(2,1)} %weight.1, bf16[128,3072]{1,0:T(8,128)(2,1)} %bitcast.9, s32[1,1024]{1,0:T(1,128)} %bitcast.13, s32[16,6]{1,0:T(8,128)} %copy.9.window), custom_call_target="tpu_custom_call" | custom-call | tf_op jit(solution)/shard_map/pallas_call | solution.py:327
  107.1 2.1 %copy.13 = bf16[1,1,128,3072]{3,2,1,0:T(8,128)(2,1)} copy(bf16[1,1,128,3072]{3,2,1,0:T(8,128)(2,1)} %bitcast.8) | data formatting | bytes 1572864
  109.1 1.6 %copy.14 = f32[384,96]{0,1:T(8,128)} copy(f32[384,96]{0,1:T(8,128)} %bitcast.10) | data formatting | bytes 294912
  110.7 1.3 %copy.15 = f32[1,1,3072]{2,1,0:T(1,128)} copy(f32[1,1,3072]{2,1,0:T(1,128)} %bitcast.11) | data formatting | bytes 24576

commit v2 on v1

--- a/solution.py
+++ b/solution.py
@@ -94,31 +94,67 @@
 
     slot_tile = lax.broadcasted_iota(jnp.int32, (NQ * rows, HEAD), 0) >> 6
     in_tile = jnp.where(slot_tile == lax.broadcasted_iota(jnp.int32, (NQ * rows, HEAD), 1), 1.0, 0.0).astype(BF)
-    tiles = window.shape[0]
-    tile_ids = lax.broadcasted_iota(jnp.int32, (tiles, HEAD), 1)
-    chosen = tile_ids == window[:, 0:1]
-    for k in range(1, window.shape[1]):
-        chosen = jnp.logical_or(chosen, tile_ids == window[:, k : k + 1])
+    tiles = window.shape[1]
+    tile_ids = lax.broadcasted_iota(jnp.int32, (HEAD, tiles), 0)
+    chosen = tile_ids == window[0:1, :]
+    for k in range(1, window.shape[0]):
+        chosen = jnp.logical_or(chosen, tile_ids == window[k : k + 1, :])
     bias = jnp.where(chosen, 0.0, MASKED)
-    bias = jnp.concatenate([bias, jnp.zeros((HEAD - tiles, HEAD), F32)], axis=0).astype(BF)
+    bias = jnp.concatenate([bias, jnp.zeros((HEAD, HEAD - tiles), F32)], axis=1).astype(BF)
     for part_of in range(NY):
         here = pl.ds(part_of * 2 * rows, 2 * rows)
         tokens = lax.broadcasted_iota(jnp.int32, (2 * rows, NQ * rows), 0) + part_of * 2 * rows
         placed = jnp.where(tokens == order[...], 1.0, 0.0).astype(BF)
         tile_of = jnp.dot(placed, in_tile, preferred_element_type=F32).astype(BF)
         kx[here, :] = tile_of
-        qx[here, :] = jnp.dot(tile_of, bias, preferred_element_type=F32).astype(BF)
+        qx[here, :] = lax.dot_general(
+            tile_of, bias, (((1,), (1,)), ((), ())), preferred_element_type=F32
+        ).astype(BF)
 
     pltpu.make_async_copy(grad, grad_v, local_sem.at[4]).wait()
-    pg[y] = (gate[...] * grad_v[...].astype(F32)).astype(BF)
+
+    def block_at(i):
+        sign = 2 * (i % 2) - 1
+        return (z + NZ + sign * (i // 2 + 1) * (1 - i // 7)) % NZ
+
+    zcols = width // NZ
+    xcols = zcols // NX
+
+    def cotangent(i, carry):
+        cols = pl.ds(pl.multiple_of(block_at(i) * zcols, HEAD), zcols)
+        pg[i, y] = (gate[:, cols] * grad_v[:, cols].astype(F32)).astype(BF)
+        return carry
+
+    lax.fori_loop(0, NZ, cotangent, 0)
+
+    left, right, far = (y + NY - 1) % NY, (y + 1) % NY, (y + 2) % NY
+    half = rows // 2
+
+    def spread(m):
+        own_rows = pg.at[pl.ds(2 * m, 2), y]
+        send(own_rows, own_rows, ag_s.at[0, m], ag_r.at[0, m], at_y(1))
+        send(own_rows, own_rows, ag_s.at[1, m], ag_r.at[1, m], at_y(NY - 1))
+
+    def pass_on(m):
+        two = pl.ds(2 * m, 2)
+        landed(pg.at[two, left], ag_r.at[0, m])
+        upper = pg.at[two, left, pl.ds(0, half)]
+        send(upper, upper, ag_s.at[2, m], ag_r.at[2, m], at_y(1))
+        landed(pg.at[two, right], ag_r.at[1, m])
+        lower = pg.at[two, right, pl.ds(half, half)]
+        send(lower, lower, ag_s.at[3, m], ag_r.at[3, m], at_y(NY - 1))
+
+    def spread_done(m):
+        landed(pg.at[pl.ds(2 * m, 2), far, pl.ds(0, half)], ag_r.at[2, m])
+        landed(pg.at[pl.ds(2 * m, 2), far, pl.ds(half, half)], ag_r.at[3, m])
 
     scale = 1.0 / math.sqrt(HEAD)
     for head in range(HEADS_HERE):
         landed(qkv_v.at[head, :, pl.ds(0, (NQ - 1) * rows), :], a2a_r.at[head])
         landed(qkv_v.at[head, :, pl.ds(0, rows), :], local_sem.at[head])
         if head == HEADS_HERE - 1:
-            send(pg.at[y], pg.at[y], ag_s.at[0], ag_r.at[0], at_y(1))
-            send(pg.at[y], pg.at[y], ag_s.at[1], ag_r.at[1], at_y(NY - 1))
+            spread(0)
+            spread(1)
 
         def attend(chunk, carry):
             here = pl.ds(pl.multiple_of(chunk * 2 * rows, 2 * rows), 2 * rows)
@@ -146,36 +182,31 @@
 
         lax.fori_loop(0, NY, attend, 0)
 
-    left, right = (y + NY - 1) % NY, (y + 1) % NY
-    half = rows // 2
-    landed(pg.at[left], ag_r.at[0])
-    send(pg.at[left, pl.ds(0, half)], pg.at[left, pl.ds(0, half)], ag_s.at[2], ag_r.at[2], at_y(1))
-    landed(pg.at[right], ag_r.at[1])
-    send(pg.at[right, pl.ds(half, half)], pg.at[right, pl.ds(half, half)], ag_s.at[3], ag_r.at[3], at_y(NY - 1))
+    pass_on(0)
+    spread(2)
+    pass_on(1)
+    spread(3)
+    pass_on(2)
+    pass_on(3)
 
     landed(w_v.at[pl.ds(0, feats), :], local_sem.at[3])
     landed(w_v.at[pl.ds(0, feats), :], w_r)
     for head in range(HEADS_HERE):
         landed(att_r.at[:, :, pl.ds(0, 2 * HEAD)], swap_r.at[head])
 
-    def project(tile, carry):
+    def project(i, carry):
+        tile = 3 * (i // 3 % 2 * 2 + i // 6) + i % 3
         cols = pl.ds(pl.multiple_of(tile * 256, 256), 256)
         part[:, :, cols] = jnp.dot(
             att_r[...].reshape(NY * rows, 2 * feats), w_v[:, cols], preferred_element_type=F32
         ).reshape(NY, rows, 256)
         return carry
 
-    lax.fori_loop(0, width // 256, project, 0)
-
-    far = (y + 2) % NY
-    landed(pg.at[far, pl.ds(0, half)], ag_r.at[2])
-    landed(pg.at[far, pl.ds(0, half)], ag_r.at[3])
-
     group = width // 4
     first_column = (0, 2 * group, group, 3 * group)
 
-    def y_step(k):
-        for ch in range(4):
+    def y_step(k, pair):
+        for ch in (2 * pair, 2 * pair + 1):
             up = ch % 2 == 0
             block = (y + 2 * NY - 1 - k) % NY if up else (y + 1 + k) % NY
             cols = pl.ds(first_column[ch], group)
@@ -190,19 +221,14 @@
                 )
             else:
                 gated_out[:, cols] = (gate[:, cols] * value).astype(BF)
-                gg[q, :, cols] = jnp.sum(grad_v[:, cols].astype(F32) * value, axis=0, keepdims=True)
-
-    y_step(0)
-
-    zcols = width // NZ
-    xcols = zcols // NX
+                gg[pair, q, :, pl.ds(ch % 2 * group, group)] = jnp.sum(
+                    grad_v[:, cols].astype(F32) * value, axis=0, keepdims=True
+                )
 
     def wgrad(i, carry):
-        sign = 2 * (i % 2) - 1
-        block = (z + NZ + sign * (i // 2 + 1) * (1 - i // 7)) % NZ
-        cols = pl.ds(pl.multiple_of(block * zcols, HEAD), zcols)
+        block = block_at(i)
         product = lax.dot_general(
-            pg[:, :, cols].reshape(NY * rows, zcols),
+            pg[i].reshape(NY * rows, zcols),
             att_r[...].reshape(NY * rows, 2 * feats),
             (((0,), (0,)), ((), ())),
             preferred_element_type=F32,
@@ -239,31 +265,44 @@
             else:
                 xown[...] = value
 
-    lax.fori_loop(0, 4, wgrad, 0)
+    def gate_sums(pair):
+        def one_peer(k, carry):
+            send(gg.at[pair, q], gg.at[pair, q], gg_s, gg_r.at[pair], at_seq((q + k) % NQ))
+            return carry
+
+        lax.fori_loop(1, NQ, one_peer, 0)
+
+    def project_pair(pair):
+        lax.fori_loop(6 * pair, 6 * pair + 6, project, 0)
+
+    spread_done(0)
+    lax.fori_loop(0, 2, wgrad, 0)
+    spread_done(1)
+    lax.fori_loop(2, 4, wgrad, 0)
     z_step(0)
-    lax.fori_loop(4, 8, wgrad, 0)
+    project_pair(0)
+    y_step(0, 0)
     z_step(1)
-    y_step(1)
+    project_pair(1)
+    y_step(0, 1)
+    spread_done(2)
+    lax.fori_loop(4, 6, wgrad, 0)
+    spread_done(3)
+    lax.fori_loop(6, 8, wgrad, 0)
     z_step(2)
+    y_step(1, 0)
     z_step(3)
-    y_step(2)
+    y_step(1, 1)
     z_step(4)
     z_step(5)
-    y_step(3)
-
-    def gate_sums(k, carry):
-        send(gg.at[q], gg.at[q], gg_s, gg_r, at_seq((q + k) % NQ))
-        return carry
-
-    lax.fori_loop(1, NQ, gate_sums, 0)
+    y_step(2, 0)
     z_step(6)
+    y_step(2, 1)
     z_step(7)
-
-    landed(gg.at[pl.ds(0, NQ - 1)], gg_r)
-    total = gg[0]
-    for k in range(1, NQ):
-        total = total + gg[k]
-    ggrad_out[...] = total
+    y_step(3, 0)
+    gate_sums(0)
+    y_step(3, 1)
+    gate_sums(1)
 
     value = xown[...]
     for j in range(NX - 1):
@@ -271,21 +310,36 @@
         value = value + xr[j].astype(F32)
     wgrad_out[...] = value
 
+    for pair in range(2):
+        landed(gg.at[0, pl.ds(0, NQ - 1)], gg_r.at[pair])
+        total = gg[pair, 0]
+        for k in range(1, NQ):
+            total = total + gg[pair, k]
+        for side in range(2):
+            ggrad_out[:, pl.ds(first_column[2 * pair + side], group)] = total[:, side * group : (side + 1) * group]
+
     landed(qkv_v.at[:, :, pl.ds(0, (NQ - 1) * rows), :], a2a_s)
     landed(att_v, swap_s)
     landed(w_v.at[pl.ds(0, feats), :], w_s)
-    for k in range(2):
-        landed(pg.at[0], ag_s.at[k])
-        landed(pg.at[0, pl.ds(0, half)], ag_s.at[2 + k])
+    for m in range(NZ // 2):
+        for k in range(2):
+            landed(pg.at[pl.ds(0, 2), 0], ag_s.at[k, m])
+            landed(pg.at[pl.ds(0, 2), 0, pl.ds(0, half)], ag_s.at[2 + k, m])
     for ch in range(4):
         for k in range(NY - 1):
             landed(rs_s.at[ch, k], y_s.at[ch, k])
         for k in range(NZ - 1):
             landed(zs.at[ch, k], z_s.at[ch, k])
-    landed(gg.at[pl.ds(0, NQ - 1)], gg_s)
+    landed(gg.at[:, pl.ds(0, NQ - 1)], gg_s)
     landed(ex_s, ex_ss)
     for j in range(NX - 1):
         landed(xs.at[j], x_s.at[j])
+
+
+def finish(gated, wgrad, ggrad, gated_out, wgrad_out, ggrad_out):
+    gated_out[...] = gated[...]
+    ggrad_out[...] = ggrad[...]
+    wgrad_out[...] = wgrad[...]
 
 
 def per_device(qkv_rows, gate, out_weight, out_grad, tile_order, window):
@@ -307,11 +361,11 @@
         pltpu.VMEM((NY, rows, 2 * feats), BF),
         pltpu.VMEM((2 * feats, width), BF),
         pltpu.VMEM((rows, width), BF),
-        pltpu.VMEM((NY, rows, width), BF),
+        pltpu.VMEM((NZ, NY, rows, zcols), BF),
         pltpu.VMEM((NY, rows, width), F32),
         pltpu.VMEM((4, NY - 1, rows, group), BF),
         pltpu.VMEM((4, NY - 1, rows, group), BF),
-        pltpu.VMEM((NQ, 1, width), F32),
+        pltpu.VMEM((2, NQ, 1, width // 2), F32),
         pltpu.VMEM((NZ, NX, xcols, feats), F32),
         pltpu.VMEM((NZ, NX, xcols, feats), BF),
         pltpu.VMEM((NZ, NX, xcols, feats), BF),
@@ -321,7 +375,7 @@
         pltpu.VMEM((NX - 1, xcols, feats), BF),
         pltpu.VMEM((xcols, feats), F32),
         dma((5,)), dma(()), dma((HEADS_HERE,)), dma(()), dma((HEADS_HERE,)), dma(()), dma(()),
-        dma((4,)), dma((4,)), dma((4, NY - 1)), dma((4, NY - 1)), dma(()), dma(()), dma(()), dma((NZ,)),
+        dma((4, NZ // 2)), dma((4, NZ // 2)), dma((4, NY - 1)), dma((4, NY - 1)), dma(()), dma((2,)), dma(()), dma((NZ,)),
         dma((4, NZ - 1)), dma((4, NZ - 1)), dma((NX - 1,)), dma((NX - 1,)),
     ]
     gated_out, wgrad, ggrad = pl.pallas_call(
@@ -343,8 +397,18 @@
         out_weight,
         out_grad.reshape(rows, width),
         tile_order.reshape(1, tokens),
-        window,
+        window.T,
     )
+    gated_out, wgrad, ggrad = pl.pallas_call(
+        finish,
+        out_shape=(
+            jax.ShapeDtypeStruct((rows, width), BF),
+            jax.ShapeDtypeStruct((xcols, feats), F32),
+            jax.ShapeDtypeStruct((1, width), F32),
+        ),
+        in_specs=[vmem, vmem, vmem],
+        out_specs=(vmem, vmem, vmem),
+    )(gated_out, wgrad, ggrad)
     return (
         gated_out.reshape(1, 1, rows, width),
         wgrad.T,

time: 114 us -> 108 us (0.947); the launches traced: 112 us -> 108 us
  local copies, waits for them, and re-layouts: 6.31 us -> 0 us
  Pallas kernels: 105 us -> 107 us
    unnamed x4 -> x0, local copies, waits for them, and re-layouts: 6.31 us -> none
    pallas_call x0 -> x1, Pallas kernels: none -> 2.16 us  [per_device(): pl.pallas_call(finish, out_shape=(jax.ShapeDtypeStruct((rows, width), BF)...]
where the time goes in v2:
time: 108 us
  Pallas kernels  107 us (99%)
    pallas_call x1, Pallas kernels, per_device(): pl.pallas_call(kernel, out_shape=(jax.ShapeDtypeStruct((rows, width), BF)...  105 us
    pallas_call x1, Pallas kernels, per_device(): pl.pallas_call(finish, out_shape=(jax.ShapeDtypeStruct((rows, width), BF)...  2.16 us

profile of v2, /device:TPU:1, one launch (start us, length us, event | category | flops | bytes accessed | tf_op | source)
XLA Modules:
  0.0 108.1 jit_solution(2657637255887070562)
XLA Ops:
  0.6 105.3 %shard_map.85 = (bf16[128,3072]{1,0:T(8,128)(2,1)}, f32[96,384]{1,0:T(8,128)}, f32[1,3072]{1,0:T(1,128)}) custom-call(bf16[128,9216]{1,0:T(8,128)(2,1)} %bitcast.8, f32[1,3072]{1,0:T(1,128)} %bitcast.10, bf16[384,3072]{1,0:T(8,128)(2,1)} %weight.1, bf16[128,3072]{1,0:T(8,128)(2,1)} %bitcast.9, s32[1,1024]{1,0:T(1,128)} %bitcast.11, s32[6,16]{1,0:T(8,128)} %bitcast.12), custom_call_target="tpu_custom_call" | custom-call | tf_op jit(solution)/shard_map/pallas_call | solution.py:381
  105.9 2.2 %shard_map.86 = (bf16[128,3072]{1,0:T(8,128)(2,1)}, f32[96,384]{1,0:T(8,128)}, f32[1,3072]{1,0:T(1,128)}) custom-call(bf16[128,3072]{1,0:T(8,128)(2,1)} %get-tuple-element.9.gated, f32[96,384]{1,0:T(8,128)} %get-tuple-element.10.wgrad, f32[1,3072]{1,0:T(1,128)} %get-tuple-element.11.ggrad), custom_call_target="tpu_custom_call" | custom-call | tf_op jit(solution)/shard_map/pallas_call | solution.py:402

commit v3 on v2

--- a/solution.py
+++ b/solution.py
@@ -114,8 +114,7 @@
     pltpu.make_async_copy(grad, grad_v, local_sem.at[4]).wait()
 
     def block_at(i):
-        sign = 2 * (i % 2) - 1
-        return (z + NZ + sign * (i // 2 + 1) * (1 - i // 7)) % NZ
+        return (z + NZ + (1 - 2 * (i % 2)) * (NZ // 2 - (i + 1) // 2)) % NZ
 
     zcols = width // NZ
     xcols = zcols // NX
@@ -150,11 +149,11 @@
 
     scale = 1.0 / math.sqrt(HEAD)
     for head in range(HEADS_HERE):
+        if head == HEADS_HERE - 1:
+            for m in range(NZ // 2):
+                spread(m)
         landed(qkv_v.at[head, :, pl.ds(0, (NQ - 1) * rows), :], a2a_r.at[head])
         landed(qkv_v.at[head, :, pl.ds(0, rows), :], local_sem.at[head])
-        if head == HEADS_HERE - 1:
-            spread(0)
-            spread(1)
 
         def attend(chunk, carry):
             here = pl.ds(pl.multiple_of(chunk * 2 * rows, 2 * rows), 2 * rows)
@@ -183,9 +182,7 @@
         lax.fori_loop(0, NY, attend, 0)
 
     pass_on(0)
-    spread(2)
     pass_on(1)
-    spread(3)
     pass_on(2)
     pass_on(3)
 
@@ -243,27 +240,38 @@
 
     z_chains = ((2, 1), (3, -1), (1, 1), (0, -1))
 
+    far_hops = NZ // 2
+
     def z_step(k):
-        if k < 4:
-            exchanged(2 * k)
-            exchanged(2 * k + 1)
+        for i in ((0, 1, 2), (3, 4), (5, 6), (), (7,))[k]:
+            exchanged(i)
         for ch, (j, way) in enumerate(z_chains):
             xb = (x + j) % NX
-            block = (z + 2 * NZ - way * (1 + k)) % NZ
-            value = own[block, xb] + ex_r[block, xb].astype(F32)
-            if k > 0:
-                landed(zr.at[ch, k - 1], z_r.at[ch, k - 1])
-                value = value + zr[ch, k - 1].astype(F32)
-            if k < NZ - 1:
-                zs[ch, k] = value.astype(BF)
+            if k == far_hops:
+                value = own[z, xb] + ex_r[z, xb].astype(F32)
+                for slot in (far_hops - 1, NZ - 2):
+                    landed(zr.at[ch, slot], z_r.at[ch, slot])
+                    value = value + zr[ch, slot].astype(F32)
+                if j > 0:
+                    xs[j - 1] = value.astype(BF)
+                    send(xs.at[j - 1], xr.at[j - 1], x_s.at[j - 1], x_r.at[j - 1], at_x(j))
+                else:
+                    xown[...] = value
+                continue
+            for hops, first, towards in ((far_hops, 0, way), (far_hops - 1, far_hops, -way)):
+                if k >= hops:
+                    continue
+                block = (z + NZ + towards * (hops - k)) % NZ
+                slot = first + k
+                value = own[block, xb] + ex_r[block, xb].astype(F32)
+                if k > 0:
+                    landed(zr.at[ch, slot - 1], z_r.at[ch, slot - 1])
+                    value = value + zr[ch, slot - 1].astype(F32)
+                zs[ch, slot] = value.astype(BF)
                 send(
-                    zs.at[ch, k], zr.at[ch, k], z_s.at[ch, k], z_r.at[ch, k], at_z(1 if way > 0 else NZ - 1)
+                    zs.at[ch, slot], zr.at[ch, slot], z_s.at[ch, slot], z_r.at[ch, slot],
+                    at_z(1 if towards > 0 else NZ - 1),
                 )
-            elif j > 0:
-                xs[j - 1] = value.astype(BF)
-                send(xs.at[j - 1], xr.at[j - 1], x_s.at[j - 1], x_r.at[j - 1], at_x(j))
-            else:
-                xown[...] = value
 
     def gate_sums(pair):
         def one_peer(k, carry):
@@ -279,30 +287,27 @@
     lax.fori_loop(0, 2, wgrad, 0)
     spread_done(1)
     lax.fori_loop(2, 4, wgrad, 0)
-    z_step(0)
     project_pair(0)
     y_step(0, 0)
-    z_step(1)
+    z_step(0)
     project_pair(1)
     y_step(0, 1)
     spread_done(2)
     lax.fori_loop(4, 6, wgrad, 0)
     spread_done(3)
     lax.fori_loop(6, 8, wgrad, 0)
+    y_step(1, 0)
+    z_step(1)
+    y_step(1, 1)
     z_step(2)
-    y_step(1, 0)
+    y_step(2, 0)
+    y_step(2, 1)
     z_step(3)
-    y_step(1, 1)
-    z_step(4)
-    z_step(5)
-    y_step(2, 0)
-    z_step(6)
-    y_step(2, 1)
-    z_step(7)
     y_step(3, 0)
     gate_sums(0)
     y_step(3, 1)
     gate_sums(1)
+    z_step(4)
 
     value = xown[...]
     for j in range(NX - 1):

time: 108 us -> 101 us (0.935); the launches traced: 108 us -> 99.5 us
  Pallas kernels: 107 us -> 98.8 us
    pallas_call x1, Pallas kernels: 105 us -> 96.7 us  [per_device(): pl.pallas_call(kernel, out_shape=(jax.ShapeDtypeStruct((rows, width), BF)...]
where the time goes in v3:
time: 101 us; the launch traced here: 99.5 us
  Pallas kernels  98.8 us (98%)
    pallas_call x1, Pallas kernels, per_device(): pl.pallas_call(kernel, out_shape=(jax.ShapeDtypeStruct((rows, width), BF)...  96.7 us
    pallas_call x1, Pallas kernels, per_device(): pl.pallas_call(finish, out_shape=(jax.ShapeDtypeStruct((rows, width), BF)...  2.16 us

profile of v3, /device:TPU:1, one launch (start us, length us, event | category | flops | bytes accessed | tf_op | source)
XLA Modules:
  0.0 99.5 jit_solution(15864336617179771383)
XLA Ops:
  0.6 96.7 %shard_map.85 = (bf16[128,3072]{1,0:T(8,128)(2,1)}, f32[96,384]{1,0:T(8,128)}, f32[1,3072]{1,0:T(1,128)}) custom-call(bf16[128,9216]{1,0:T(8,128)(2,1)} %bitcast.8, f32[1,3072]{1,0:T(1,128)} %bitcast.10, bf16[384,3072]{1,0:T(8,128)(2,1)} %weight.1, bf16[128,3072]{1,0:T(8,128)(2,1)} %bitcast.9, s32[1,1024]{1,0:T(1,128)} %bitcast.11, s32[6,16]{1,0:T(8,128)} %bitcast.12), custom_call_target="tpu_custom_call" | custom-call | tf_op jit(solution)/shard_map/pallas_call | solution.py:386
  97.3 2.2 %shard_map.86 = (bf16[128,3072]{1,0:T(8,128)(2,1)}, f32[96,384]{1,0:T(8,128)}, f32[1,3072]{1,0:T(1,128)}) custom-call(bf16[128,3072]{1,0:T(8,128)(2,1)} %get-tuple-element.9.gated, f32[96,384]{1,0:T(8,128)} %get-tuple-element.10.wgrad, f32[1,3072]{1,0:T(1,128)} %get-tuple-element.11.ggrad), custom_call_target="tpu_custom_call" | custom-call | tf_op jit(solution)/shard_map/pallas_call | solution.py:407
